TPU v7x, 512 devices: a whole 4x8x8 slice. The times are simulated.
512 devices in a mesh: sp: 128 (over y, z, core), tp: 4 (over x).
Axes of the slice: x: 4, y: 8, z: 8, core: 2. Of those that a mesh axis runs over, the one named last changes fastest.
Arguments:
- prefilled_block_keys: bfloat16 [8192, 8, 1024], P(('sp', 'tp')), may hold values from -4 to 4
- prefilled_block_values: bfloat16 [8192, 8, 1024], P(('sp', 'tp')), may hold values from -6 to 6
- queries: bfloat16 [4, 4, 8192], P(None, None, 'tp'), may hold values from -128 to 128
- step_token_keys: bfloat16 [4, 4, 1024], P(None, None, 'tp'), may hold values from -32 to 32
- step_token_values: bfloat16 [4, 4, 1024], P(None, None, 'tp'), may hold values from -6 to 6
- lengths: int32 [4], replicated, may hold values from 8185 to 40960, as said below
- block_request: int32 [8192], P(('sp', 'tp')), may hold values from 0 to 3, as said below
- block_number: int32 [8192], P(('sp', 'tp')), may hold values from 0 to 5119
- owner_rank: int32 [8192], P(('sp', 'tp')), may hold values from 0 to 79, as said below
- owner_slot: int32 [8192], P(('sp', 'tp')), may hold values from 0 to 127, as said below
- group_first: int32 [4], replicated, may hold values from 0 to 112, as said below
Outputs:
- attended: float32 [4, 4, 8192], P(None, None, 'tp')
- log_norm: float32 [4, 4, 64], P(None, None, 'tp')
- owner_slot_keys: bfloat16 [16384, 8, 1024], P('sp', None, 'tp')
- owner_slot_values: bfloat16 [16384, 8, 1024], P('sp', None, 'tp')
Inputs may be any that keep to these rules, and one draw needn't show every extreme that they name: `lengths`: each request's length lies in its last block: with n blocks, 8 * (n - 1) < length <= 8 * n. `block_request`: every request has blocks, and its blocks carry the numbers 0 to n - 1 once each. The owner group_first + owner_rank lies in the request's group. `owner_slot`: no two blocks share an owner and a slot; the 64 blocks of one index of sp in the prefill layout reach one owner at most 1 times, and this is reached. `group_first`: the groups are runs of indices of sp, one for each request in some order, that do not meet and cover the whole axis.
All inputs are finite; a program needn't handle non-finite values.
Results may differ from a plain program's by a relative error of at most 0.0004.
Values may be sent and summed in bfloat16 or wider, within the bound.
A program may use at most 64 MiB of HBM per device.

v0:
```python
import math
import jax
import jax.numpy as jnp
from jax import lax
from jax.sharding import PartitionSpec as P

HEAD_SIZE = 128
NEGATIVE = -1e30


def lookup(small_table, indices):
    hits = indices[..., None] == jnp.arange(small_table.shape[0], dtype=jnp.int32)
    return jnp.sum(jnp.where(hits, small_table, 0), axis=-1)


def earlier_same(owners):
    width_count = owners.shape[-1]
    alike = owners[..., :, None] == owners[..., None, :]
    before = jnp.arange(width_count)[None, :] < jnp.arange(width_count)[:, None]
    return jnp.sum(alike & before, axis=-1)


def attend(
    key_blocks,
    value_blocks,
    token_request,
    token_position,
    queries,
    step_token_keys,
    step_token_values,
    lengths,
):
    steps, requests, query_width = queries.shape
    kv_local = key_blocks.shape[-1] // HEAD_SIZE
    queries_per_group = query_width // HEAD_SIZE // kv_local
    tokens = key_blocks.shape[0] * key_blocks.shape[1]
    score_scale = 1.0 / math.sqrt(HEAD_SIZE)
    key_matrix = key_blocks.reshape(tokens, kv_local, HEAD_SIZE)
    value_matrix = value_blocks.reshape(tokens, kv_local, HEAD_SIZE)
    query_matrix = queries.reshape(steps, requests, kv_local, queries_per_group, HEAD_SIZE)
    current_keys = step_token_keys.reshape(steps, requests, kv_local, HEAD_SIZE)
    current_values = step_token_values.reshape(steps, requests, kv_local, HEAD_SIZE)
    within_length = token_position < lookup(lengths, token_request)
    allowed_mask = (
        token_request[None, :] == jnp.arange(requests, dtype=jnp.int32)[:, None]
    ) & within_length[None, :]
    cache_allowed = allowed_mask[None, :, None, None, :]
    causal = (jnp.arange(steps)[None, :] <= jnp.arange(steps)[:, None])[:, None, None, None, :]
    scores = (
        jnp.einsum("srhgd,thd->srhgt", query_matrix, key_matrix, preferred_element_type=jnp.float32)
        * score_scale
    )
    fresh_scores = (
        jnp.einsum(
            "srhgd,jrhd->srhgj", query_matrix, current_keys, preferred_element_type=jnp.float32
        )
        * score_scale
    )
    local_top = jnp.maximum(
        jnp.max(jnp.where(cache_allowed, scores, NEGATIVE), axis=-1),
        jnp.max(jnp.where(causal, fresh_scores, NEGATIVE), axis=-1),
    )
    row_top = lax.pmax(local_top, "sp")
    weights = jnp.where(cache_allowed, jnp.exp(scores - row_top[..., None]), 0.0)
    weight_sum = jnp.sum(weights, axis=-1)
    numerator = jnp.einsum(
        "srhgt,thd->srhgd",
        weights.astype(jnp.bfloat16),
        value_matrix,
        preferred_element_type=jnp.float32,
    )
    numerator, weight_sum = lax.psum((numerator, weight_sum), "sp")
    fresh_weights = jnp.where(causal, jnp.exp(fresh_scores - row_top[..., None]), 0.0)
    totals = weight_sum + jnp.sum(fresh_weights, axis=-1)
    numerator = numerator + jnp.einsum(
        "srhgj,jrhd->srhgd",
        fresh_weights.astype(jnp.bfloat16),
        current_values,
        preferred_element_type=jnp.float32,
    )
    attended = (numerator / totals[..., None]).reshape(steps, requests, query_width)
    log_norm = (row_top + jnp.log(totals)).reshape(steps, requests, kv_local * queries_per_group)
    return (attended, log_norm)


def on_device(
    prefilled_block_keys,
    prefilled_block_values,
    queries,
    step_token_keys,
    step_token_values,
    lengths,
    block_request,
    block_number,
    owner_rank,
    owner_slot,
    group_first,
):
    sp_count = lax.axis_size("sp")
    tp_count = lax.axis_size("tp")
    own_blocks, block_len, full_width = prefilled_block_keys.shape
    piece_width = full_width // tp_count
    row_blocks = own_blocks * tp_count
    slot_count = 2 * row_blocks
    pair_cap = max(1, slot_count // sp_count)
    my_row = lax.axis_index("sp")
    block_tables = jnp.stack([block_request, block_number, owner_rank, owner_slot], axis=1)
    gathered = lax.all_gather(block_tables, ("sp", "tp"), axis=0, tiled=True).reshape(
        sp_count, row_blocks, 4
    )
    all_owner = lookup(group_first, gathered[..., 0]) + gathered[..., 2]
    split_keys = prefilled_block_keys.reshape(own_blocks, block_len, tp_count, piece_width)
    split_values = prefilled_block_values.reshape(own_blocks, block_len, tp_count, piece_width)
    row_keys, row_values = (
        lax.all_to_all(split_keys, "tp", split_axis=2, concat_axis=0, tiled=True),
        lax.all_to_all(split_values, "tp", split_axis=2, concat_axis=0, tiled=True),
    )
    row_keys = row_keys.reshape(row_blocks, block_len, piece_width)
    row_values = row_values.reshape(row_blocks, block_len, piece_width)
    row_owner = lax.dynamic_index_in_dim(all_owner, my_row, 0, keepdims=False)
    send_index = row_owner * pair_cap + earlier_same(row_owner)
    wanted = send_index[None, :] == jnp.arange(sp_count * pair_cap, dtype=jnp.int32)[:, None]
    source = jnp.sum(jnp.where(wanted, jnp.arange(row_blocks, dtype=jnp.int32)[None, :], 0), axis=1)
    present = jnp.any(wanted, axis=1)[:, None, None]
    empty_value = jnp.zeros((), jnp.bfloat16)
    send_keys = jnp.where(present, jnp.take(row_keys, source, axis=0), empty_value)
    send_values = jnp.where(present, jnp.take(row_values, source, axis=0), empty_value)
    got_keys, got_values = (
        lax.all_to_all(send_keys, "sp", split_axis=0, concat_axis=0, tiled=True),
        lax.all_to_all(send_values, "sp", split_axis=0, concat_axis=0, tiled=True),
    )
    incoming = jnp.arange(sp_count, dtype=jnp.int32)[:, None] * pair_cap + earlier_same(all_owner)
    owned_here = (all_owner == my_row).reshape(-1)
    matches = owned_here[None, :] & (
        gathered[..., 3].reshape(-1)[None, :] == jnp.arange(slot_count, dtype=jnp.int32)[:, None]
    )
    arrival = jnp.sum(jnp.where(matches, incoming.reshape(-1)[None, :], 0), axis=1)
    filled = jnp.any(matches, axis=1)
    slot_request = jnp.where(
        filled, jnp.sum(jnp.where(matches, gathered[..., 0].reshape(-1)[None, :], 0), axis=1), -1
    )
    slot_number = jnp.sum(jnp.where(matches, gathered[..., 1].reshape(-1)[None, :], 0), axis=1)
    owner_slot_keys = jnp.where(
        filled[:, None, None], jnp.take(got_keys, arrival, axis=0), empty_value
    )
    owner_slot_values = jnp.where(
        filled[:, None, None], jnp.take(got_values, arrival, axis=0), empty_value
    )
    offsets = jnp.arange(block_len, dtype=jnp.int32)[None, :]
    token_request = jnp.repeat(slot_request, block_len, total_repeat_length=slot_count * block_len)
    token_position = (slot_number[:, None] * block_len + offsets).reshape(-1)
    attended, log_norm = attend(
        owner_slot_keys,
        owner_slot_values,
        token_request,
        token_position,
        queries,
        step_token_keys,
        step_token_values,
        lengths,
    )
    return (attended, log_norm, owner_slot_keys, owner_slot_values)


def solution(mesh):
    return jax.shard_map(
        on_device,
        mesh=mesh,
        in_specs=(
            P(("sp", "tp"), None, None),
            P(("sp", "tp"), None, None),
            P(None, None, "tp"),
            P(None, None, "tp"),
            P(None, None, "tp"),
            P(),
            P(("sp", "tp")),
            P(("sp", "tp")),
            P(("sp", "tp")),
            P(("sp", "tp")),
            P(),
        ),
        out_specs=(
            P(None, None, "tp"),
            P(None, None, "tp"),
            P("sp", None, "tp"),
            P("sp", None, "tp"),
        ),
        check_vma=False,
    )
```

profile of v0, /device:TPU:1, one launch (start us, length us, event | category | flops | bytes accessed | tf_op | source)
XLA Modules:
  0.0 1391.8 jit_solution(11877630832900269052)
XLA Ops:
  7.2 1.7 copy.174
  8.9 4.8 all-to-all-start.2
  13.8 132.5 %all-gather = s32[512,16,4]{1,2,0:T(4,128)S(1)} all-gather(s32[1,16,4]{1,2,0:T(4,128)S(1)} %add_bitcast_fusion), channel_id=1, replica_groups=mesh['sp'=128,'tp'=4] {'sp','tp'}, dimensions={0}, use_global_device_ids=true | all-gather | bytes 131328 | tf_op jit(solution)/shard_map/all_gather | solution.py:108
  148.2 0.7 copy.175
  148.9 0.7 convert_reduce_fusion
  150.2 2.5 select_reduce_fusion
  152.7 3.4 all-to-all-start
  156.2 0.6 fusion.1
  156.8 0.7 gather_fusion.3
  157.5 4.2 all-to-all-done
  162.3 1.5 select_select_fusion.3
  163.8 11.1 all-to-all-start.3
  175.0 6.6 gather_fusion
  181.9 12.5 all-to-all-done.3
  194.4 7.2 all-to-all-start.1
  203.3 18.0 %all-to-all-done.1 = bf16[128,8,256]{2,1,0:T(8,128)(2,1)S(1)} async-done(((bf16[128,8,256]{2,1,0:T(8,128)(2,1)}), bf16[128,8,256]{2,1,0:T(8,128)(2,1)S(1)}, u32[]{:S(2)}, u32[]{:S(2)}) %all-to-all-start.1) | async-done | bytes 524320 | tf_op jit(solution)/shard_map/all_to_all | solution.py:130
  221.9 0.7 select_select_fusion.2
  223.5 487.2 %pmax.7 = f32[4,4,2,8]{3,1,0,2:T(4,128)S(1)} all-reduce(f32[4,4,2,8]{3,1,0,2:T(4,128)S(1)} %copy_maximum_fusion), channel_id=1, replica_groups=mesh['sp'=128,'tp'=4] {'sp'}, use_global_device_ids=true, to_apply=%region_12.15 | all-reduce | flops 256 | bytes 2048 | tf_op jit(solution)/shard_map/pmax | solution.py:63
  711.0 490.9 %psum.15 = f32[4,4,2,8]{3,1,0,2:T(4,128)S(1)} all-reduce(f32[4,4,2,8]{3,1,0,2:T(4,128)S(1)} %fusion.6), channel_id=1, replica_groups=mesh['sp'=128,'tp'=4] {'sp'}, use_global_device_ids=true, to_apply=%region_15.18 | all-reduce | flops 256 | bytes 2048 | tf_op jit(solution)/shard_map/psum | solution.py:72
  1202.0 1.0 convolution_bitcast_fusion
  1203.2 0.7 reshape.291
  1203.9 179.2 %all-reduce.2.cloned.1.call-done = f32[4,4,2,8,128]{4,3,1,0,2:T(8,128)} async-done(((f32[4,4,2,8,128]{4,3,1,0,2:T(8,128)}), f32[4,4,2,8,128]{4,3,1,0,2:T(8,128)}) %all-reduce.2.cloned.1.call-update) | async-done | bytes 131088 | tf_op jit(solution)/shard_map/psum | solution.py:72
  1383.1 1.1 fusion.4
  1384.3 0.7 reshape.290
  (90 shorter events, 6.9 us)
Async XLA Ops:
  7.2 6.6 copy-start.12
  7.2 6.6 copy-start.11
  7.2 6.6 copy-start.10
  7.2 6.6 copy-start.9
  8.9 143.8 %all-to-all-start.2 = ((bf16[16,8,4,256]{3,1,0,2:T(8,128)(2,1)}), bf16[16,8,4,256]{3,1,0,2:T(8,128)(2,1)S(1)}, u32[]{:S(2)}, u32[]{:S(2)}) async-start(bf16[16,8,4,256]{3,1,0,2:T(8,128)(2,1)} %bitcast.72), calls=%async_computation.2 | async-start | bytes 524288 | tf_op jit(solution)/shard_map/all_to_all | solution.py:115
  146.3 0.7 copy-start.7
  146.3 1.8 copy-start.2
  146.7 3.4 copy-start.4
  152.7 8.9 all-to-all-start
  163.8 30.6 %all-to-all-start.3 = ((bf16[128,8,256]{2,1,0:T(8,128)(2,1)}), bf16[128,8,256]{2,1,0:T(8,128)(2,1)S(1)}, u32[]{:S(2)}, u32[]{:S(2)}) async-start(bf16[128,8,256]{2,1,0:T(8,128)(2,1)} %get-tuple-element.35), calls=%async_computation.3 | async-start | bytes 1048576 | tf_op jit(solution)/shard_map/all_to_all | solution.py:129
  175.0 6.7 copy-start.8
  181.6 20.4 %copy-start.3 = (bf16[4,4,2048]{2,1,0:T(4,128)(2,1)S(1)}, bf16[4,4,2048]{2,1,0:T(4,128)(2,1)}, u32[]{:S(2)}) copy-start(bf16[4,4,2048]{2,1,0:T(4,128)(2,1)} %param.19) | copy-start | bytes 196612
  181.6 20.5 %copy-start.5 = (bf16[4,4,256]{2,1,0:T(4,128)(2,1)S(1)}, bf16[4,4,256]{2,1,0:T(4,128)(2,1)}, u32[]{:S(2)}) copy-start(bf16[4,4,256]{2,1,0:T(4,128)(2,1)} %param.20) | copy-start | bytes 24580
  181.6 20.5 %copy-start.6 = (bf16[4,4,256]{2,1,0:T(4,128)(2,1)S(1)}, bf16[4,4,256]{2,1,0:T(4,128)(2,1)}, u32[]{:S(2)}) copy-start(bf16[4,4,256]{2,1,0:T(4,128)(2,1)} %param.21) | copy-start | bytes 24580
  194.4 26.8 %all-to-all-start.1 = ((bf16[128,8,256]{2,1,0:T(8,128)(2,1)}), bf16[128,8,256]{2,1,0:T(8,128)(2,1)S(1)}, u32[]{:S(2)}, u32[]{:S(2)}) async-start(bf16[128,8,256]{2,1,0:T(8,128)(2,1)} %get-tuple-element.34), calls=%async_computation.1 | async-start | bytes 1048576 | tf_op jit(solution)/shard_map/all_to_all | solution.py:130
  201.7 1181.4 %all-reduce.2.cloned.1.call-start = ((), (), s32[]{:S(2)}) async-start(), calls=%async_computation.4 | async-start | bytes 262144 | tf_op jit(solution)/shard_map/psum | solution.py:72
  222.7 0.8 copy-start.1
  222.7 979.2 %copy-start = (bf16[128,8,256]{2,1,0:T(8,128)(2,1)}, bf16[128,8,256]{2,1,0:T(8,128)(2,1)S(1)}, u32[]{:S(2)}) copy-start(bf16[128,8,256]{2,1,0:T(8,128)(2,1)S(1)} %get-tuple-element.32) | copy-start | bytes 1572868
Sparse Core Ops, SparseCore 0:
  1203.1 179.9 all-reduce.1
where the time goes:
time: 1390 us
  blocking collectives  1110 us (80%)
  waiting for transfers between devices  214 us (15%)
  starting transfers between devices  26.9 us (2%)
  local copies, waits for them, and re-layouts  15.3 us (1%)
  between operations  14.5 us (1%)
    psum x1, blocking collectives, attend(): numerator, weight_sum = lax.psum((numerator, weight_sum), 'sp')  491 us
    pmax x1, blocking collectives, attend(): row_top = lax.pmax(local_top, 'sp')  487 us
    psum x1, waiting for transfers between devices, attend(): numerator, weight_sum = lax.psum((numerator, weight_sum), 'sp')  179 us
    all_gather x1, blocking collectives, on_device(): lax.all_gather(block_tables, ('sp', 'tp'), axis=0, tiled=True)  132 us
  transfers between devices with their start and end apart: 5, of which 4 were waited for; matrix products, arithmetic and copies ran while one was open for 1% of the time, Pallas kernels for 0%

commit v1 on v0

--- a/solution.py
+++ b/solution.py
@@ -105,9 +105,10 @@
     pair_cap = max(1, slot_count // sp_count)
     my_row = lax.axis_index("sp")
     block_tables = jnp.stack([block_request, block_number, owner_rank, owner_slot], axis=1)
-    gathered = lax.all_gather(block_tables, ("sp", "tp"), axis=0, tiled=True).reshape(
-        sp_count, row_blocks, 4
-    )
+    gathered = jnp.concatenate(
+        lax.all_to_all(jnp.stack([block_tables] * lax.axis_size(("sp", "tp"))), ("sp", "tp"), 0, 0),
+        axis=0,
+    ).reshape(sp_count, row_blocks, 4)
     all_owner = lookup(group_first, gathered[..., 0]) + gathered[..., 2]
     split_keys = prefilled_block_keys.reshape(own_blocks, block_len, tp_count, piece_width)
     split_values = prefilled_block_values.reshape(own_blocks, block_len, tp_count, piece_width)

time: 1390 us -> 1310 us (0.942)
  blocking collectives: 1110 us -> 978 us
  waiting for transfers between devices: 214 us -> 245 us
  starting transfers between devices: 26.9 us -> 46 us
    all_gather x1 -> x0, blocking collectives: 132 us -> none  [on_device(): lax.all_gather(block_tables, ('sp', 'tp'), axis=0, tiled=True)]
    all_to_all x0 -> x1, waiting for transfers between devices: none -> 30.4 us  [on_device(): lax.all_to_all(jnp.stack([block_tables] * lax.axis_size(('sp', 'tp'))), (...]
    all_to_all x0 -> x1, starting transfers between devices: none -> 22.2 us  [on_device(): lax.all_to_all(jnp.stack([block_tables] * lax.axis_size(('sp', 'tp'))), (...]
  transfers between devices with their start and end apart: 5 -> 6, of which waited for: 4 -> 6; matrix products, arithmetic and copies ran while one was open for 1% -> 1% of each run, Pallas kernels for 0% -> 0%
where the time goes in v1:
time: 1310 us
  blocking collectives  978 us (75%)
  waiting for transfers between devices  245 us (19%)
  starting transfers between devices  46 us (4%)
  local copies, waits for them, and re-layouts  15.4 us (1%)
  between operations  14.5 us (1%)
    psum x1, blocking collectives, attend(): numerator, weight_sum = lax.psum((numerator, weight_sum), 'sp')  491 us
    pmax x1, blocking collectives, attend(): row_top = lax.pmax(local_top, 'sp')  487 us
    psum x1, waiting for transfers between devices, attend(): numerator, weight_sum = lax.psum((numerator, weight_sum), 'sp')  179 us
    all_to_all x1, waiting for transfers between devices, on_device(): lax.all_to_all(jnp.stack([block_tables] * lax.axis_size(('sp', 'tp'))), (...  30.4 us
  transfers between devices with their start and end apart: 6, of which 6 were waited for; matrix products, arithmetic and copies ran while one was open for 1% of the time, Pallas kernels for 0%

profile of v1, /device:TPU:1, one launch (start us, length us, event | category | flops | bytes accessed | tf_op | source)
XLA Modules:
  0.0 1311.0 jit_solution(13599766546651387018)
XLA Ops:
  7.2 0.7 pad_add_fusion
  7.9 1.1 stack.17
  9.0 22.2 %all-to-all-start = ((s32[512,16,4]{1,2,0:T(4,128)}), s32[512,16,4]{1,2,0:T(4,128)S(1)}, u32[]{:S(2)}, u32[]{:S(2)}) async-start(s32[512,16,4]{1,2,0:T(4,128)} %stack.17), calls=%async_computation | async-start | bytes 2097152 | tf_op jit(solution)/shard_map/all_to_all | solution.py:109
  31.4 0.7 copy.172
  32.1 0.7 copy.173
  33.3 30.4 %all-to-all-done = s32[512,16,4]{1,2,0:T(4,128)S(1)} async-done(((s32[512,16,4]{1,2,0:T(4,128)}), s32[512,16,4]{1,2,0:T(4,128)S(1)}, u32[]{:S(2)}, u32[]{:S(2)}) %all-to-all-start) | async-done | bytes 131104 | tf_op jit(solution)/shard_map/all_to_all | solution.py:109
  63.7 3.4 all-to-all-start.3
  69.0 4.3 all-to-all-done.3
  73.3 3.4 all-to-all-start.1
  77.4 4.8 all-to-all-done.1
  82.9 1.5 select_select_fusion.3
  84.4 9.6 all-to-all-start.4
  94.0 0.7 convert_reduce_fusion
  95.8 2.7 select_reduce_fusion
  98.8 6.6 gather_fusion
  105.4 8.1 all-to-all-done.4
  113.4 7.4 all-to-all-start.2
  121.8 18.6 %all-to-all-done.2 = bf16[128,8,256]{2,1,0:T(8,128)(2,1)S(1)} async-done(((bf16[128,8,256]{2,1,0:T(8,128)(2,1)}), bf16[128,8,256]{2,1,0:T(8,128)(2,1)S(1)}, u32[]{:S(2)}, u32[]{:S(2)}) %all-to-all-start.2) | async-done | bytes 524320 | tf_op jit(solution)/shard_map/all_to_all | solution.py:131
  141.1 0.7 select_select_fusion.2
  142.6 487.2 %pmax.7 = f32[4,4,2,8]{3,1,0,2:T(4,128)S(1)} all-reduce(f32[4,4,2,8]{3,1,0,2:T(4,128)S(1)} %copy_maximum_fusion), channel_id=1, replica_groups=mesh['sp'=128,'tp'=4] {'sp'}, use_global_device_ids=true, to_apply=%region_12.15 | all-reduce | flops 256 | bytes 2048 | tf_op jit(solution)/shard_map/pmax | solution.py:63
  630.1 490.9 %psum.15 = f32[4,4,2,8]{3,1,0,2:T(4,128)S(1)} all-reduce(f32[4,4,2,8]{3,1,0,2:T(4,128)S(1)} %fusion.6), channel_id=1, replica_groups=mesh['sp'=128,'tp'=4] {'sp'}, use_global_device_ids=true, to_apply=%region_15.18 | all-reduce | flops 256 | bytes 2048 | tf_op jit(solution)/shard_map/psum | solution.py:72
  1121.1 1.0 convolution_bitcast_fusion
  1123.1 179.2 %all-reduce.2.cloned.1.call-done = f32[4,4,2,8,128]{4,3,1,0,2:T(8,128)} async-done(((f32[4,4,2,8,128]{4,3,1,0,2:T(8,128)}), f32[4,4,2,8,128]{4,3,1,0,2:T(8,128)}) %all-reduce.2.cloned.1.call-update) | async-done | bytes 131088 | tf_op jit(solution)/shard_map/psum | solution.py:72
  1302.3 1.1 fusion.4
  (86 shorter events, 9.4 us)
Async XLA Ops:
  9.0 22.2 %copy-start.5 = (s32[8,128]{1,0:T(8,128)S(1)}, s32[8,128]{1,0:T(8,128)}, u32[]{:S(2)}) copy-start(s32[8,128]{1,0:T(8,128)} %constant.131.clone.1) | copy-start | bytes 12292
  9.0 22.4 %copy-start.2 = (bf16[16,8,1024]{2,1,0:T(8,128)(2,1)S(1)}, bf16[16,8,1024]{2,1,0:T(8,128)(2,1)}, u32[]{:S(2)}) copy-start(bf16[16,8,1024]{2,1,0:T(8,128)(2,1)} %param.17) | copy-start | bytes 786436
  9.0 23.1 %copy-start.3 = (bf16[16,8,1024]{2,1,0:T(8,128)(2,1)S(1)}, bf16[16,8,1024]{2,1,0:T(8,128)(2,1)}, u32[]{:S(2)}) copy-start(bf16[16,8,1024]{2,1,0:T(8,128)(2,1)} %param.18) | copy-start | bytes 786436
  9.0 54.7 %all-to-all-start = ((s32[512,16,4]{1,2,0:T(4,128)}), s32[512,16,4]{1,2,0:T(4,128)S(1)}, u32[]{:S(2)}, u32[]{:S(2)}) async-start(s32[512,16,4]{1,2,0:T(4,128)} %stack.17), calls=%async_computation | async-start | bytes 2097152 | tf_op jit(solution)/shard_map/all_to_all | solution.py:109
  31.2 1.6 copy-start.4
  31.2 1.7 copy-start.6
  31.2 1.7 copy-start.7
  63.7 9.6 all-to-all-start.3
  67.2 0.7 copy-start.8
  73.3 8.9 all-to-all-start.1
  84.4 29.0 %all-to-all-start.4 = ((bf16[128,8,256]{2,1,0:T(8,128)(2,1)}), bf16[128,8,256]{2,1,0:T(8,128)(2,1)S(1)}, u32[]{:S(2)}, u32[]{:S(2)}) async-start(bf16[128,8,256]{2,1,0:T(8,128)(2,1)} %get-tuple-element.35), calls=%async_computation.4 | async-start | bytes 1048576 | tf_op jit(solution)/shard_map/all_to_all | solution.py:130
  105.3 15.6 %copy-start.9 = (s32[4]{0:T(128)S(1)}, s32[4]{0:T(128)}, u32[]{:S(2)}) copy-start(s32[4]{0:T(128)} %param.22) | copy-start | bytes 52
  113.4 27.0 %all-to-all-start.2 = ((bf16[128,8,256]{2,1,0:T(8,128)(2,1)}), bf16[128,8,256]{2,1,0:T(8,128)(2,1)S(1)}, u32[]{:S(2)}, u32[]{:S(2)}) async-start(bf16[128,8,256]{2,1,0:T(8,128)(2,1)} %get-tuple-element.34), calls=%async_computation.2 | async-start | bytes 1048576 | tf_op jit(solution)/shard_map/all_to_all | solution.py:131
  120.9 1181.4 %all-reduce.2.cloned.1.call-start = ((), (), s32[]{:S(2)}) async-start(), calls=%async_computation.5 | async-start | bytes 262144 | tf_op jit(solution)/shard_map/psum | solution.py:72
  141.8 0.8 copy-start.1
  141.8 979.2 %copy-start = (bf16[128,8,256]{2,1,0:T(8,128)(2,1)}, bf16[128,8,256]{2,1,0:T(8,128)(2,1)S(1)}, u32[]{:S(2)}) copy-start(bf16[128,8,256]{2,1,0:T(8,128)(2,1)S(1)} %get-tuple-element.32) | copy-start | bytes 1572868
Sparse Core Ops, SparseCore 0:
  1122.3 179.9 all-reduce.1
